TPU v7x, 32 devices: a whole 2x2x4 slice. The times are simulated.
32 devices in a mesh: ia: 16 (over z, x, core), ja: 2 (over y).
Axes of the slice: x: 2, y: 2, z: 4, core: 2. Of those that a mesh axis runs over, the one named last changes fastest.
Arguments:
- position: float32 [3, 8192], P(None, ('ia', 'ja')), may hold values from -5 to 5
- velocity: float32 [3, 8192], P(None, ('ia', 'ja')), may hold values from -4 to 4
- mass: float32 [8192], P(('ia', 'ja')), may hold values from 1.2207031e-05 to 0.0012207031
Outputs:
- final_position: float32 [3, 8192], P(None, ('ia', 'ja'))
- final_velocity: float32 [3, 8192], P(None, ('ia', 'ja'))
- final_accel: float32 [3, 8192], P(None, ('ia', 'ja'))
- final_jerk: float32 [3, 8192], P(None, ('ia', 'ja'))
All inputs are finite; a program needn't handle non-finite values.
Results may differ from a plain program's by a relative error of at most 0.00017.
Values sent between devices are 32-bit elements; how exact they have to be, the bound alone decides.
A program may use at most 128 MiB of HBM per device.

v0:
```python
import jax
import jax.numpy as jnp
from jax import lax
from jax.sharding import PartitionSpec as P

STEPS = 4


soft_square = 0.0025
time_step = 0.03125


def pair_block(row_set, col_set, weight):
    offset = col_set[0:3, None, :] - row_set[0:3, :, None]
    closing = col_set[3:6, None, :] - row_set[3:6, :, None]
    square = jnp.sum(offset * offset, 0) + soft_square
    inverse = lax.rsqrt(square)
    cube = inverse * inverse * inverse * weight
    radial = 3.0 * jnp.sum(offset * closing, 0) / square
    terms = jnp.concatenate([offset * cube, (closing - radial * offset) * cube], 0)
    row_part = jnp.sum(terms * col_set[6][None, None, :], 2)
    return (row_part, -jnp.sum(terms * row_set[6][None, :, None], 1))


def add_block(total, part, start):
    current = lax.dynamic_slice_in_dim(total, start, part.shape[1], 1)
    return lax.dynamic_update_slice_in_dim(total, current + part, start, 1)


def tile_forces(row_set, col_set, row_splits, col_splits, weigher):
    row_step = row_set.shape[1] // row_splits
    col_step = col_set.shape[1] // col_splits
    start_acc = (jnp.zeros((6, row_set.shape[1]), jnp.float32),)
    start_acc = start_acc + (jnp.zeros((6, col_set.shape[1]), jnp.float32),)

    def visit(turn_index, carry):
        row_start = turn_index // col_splits * row_step
        col_start = turn_index % col_splits * col_step
        row_block = lax.dynamic_slice_in_dim(row_set, row_start, row_step, 1)
        col_block = lax.dynamic_slice_in_dim(col_set, col_start, col_step, 1)
        weight = weigher(row_start, col_start, row_step, col_step)

        def active(operand):
            return pair_block(row_block, col_block, weight)

        def passive(operand):
            empty = (jnp.zeros((6, row_step), jnp.float32),)
            empty = empty + (jnp.zeros((6, col_step), jnp.float32),)
            return empty

        parts = lax.cond(jnp.any(weight > 0.0), active, passive, 0)
        result = (add_block(carry[0], parts[0], row_start),)
        result = result + (add_block(carry[1], parts[1], col_start),)
        return result

    return lax.fori_loop(0, row_splits * col_splits, visit, start_acc)


def evaluate(position, velocity, mass):
    stars_dev = position.shape[1]
    packed = jnp.concatenate([position, velocity, mass[None, :]], 0)
    row_group = lax.axis_index("ia")
    col_group = lax.axis_index("ja")
    members = lax.axis_size("ja")
    row_set = lax.all_gather(packed, "ja", axis=1, tiled=True)
    col_set = lax.all_gather(packed, "ia", axis=1, tiled=True)

    def row_numbers(row_start, row_count):
        return row_group * members * stars_dev + row_start + jnp.arange(row_count, dtype=jnp.int32)

    def weigher(row_start, col_start, row_count, col_count):
        row_index = row_numbers(row_start, row_count)
        place = col_start + jnp.arange(col_count, dtype=jnp.int32)
        col_index = (place // stars_dev * members + col_group) * stars_dev + place % stars_dev
        return (row_index[:, None] < col_index[None, :]).astype(jnp.float32)

    row_acc, col_acc = tile_forces(row_set, col_set, 2, 8, weigher)
    col_total = lax.psum_scatter(col_acc, "ia", scatter_dimension=1, tiled=True)
    total = lax.psum_scatter(row_acc, "ja", scatter_dimension=1, tiled=True) + col_total
    return (total[0:3], total[3:6])


def per_device(position, velocity, mass):
    accel, jerk = evaluate(position, velocity, mass)
    step_sq = time_step * time_step
    for step_index in range(STEPS):
        predicted_pos = (
            position
            + time_step * velocity
            + step_sq / 2.0 * accel
            + step_sq * time_step / 6.0 * jerk
        )
        predicted_vel = velocity + time_step * accel + step_sq / 2.0 * jerk
        new_accel, new_jerk = evaluate(predicted_pos, predicted_vel, mass)
        new_velocity = (
            velocity + time_step / 2.0 * (accel + new_accel) + step_sq / 12.0 * (jerk - new_jerk)
        )
        position = (
            position
            + time_step / 2.0 * (velocity + new_velocity)
            + step_sq / 12.0 * (accel - new_accel)
        )
        velocity = new_velocity
        accel = new_accel
        jerk = new_jerk
    return (position, velocity, accel, jerk)


def solution(mesh):
    return jax.shard_map(
        per_device,
        mesh=mesh,
        in_specs=(P(None, ("ia", "ja")), P(None, ("ia", "ja")), P(("ia", "ja"))),
        out_specs=(
            P(None, ("ia", "ja")),
            P(None, ("ia", "ja")),
            P(None, ("ia", "ja")),
            P(None, ("ia", "ja")),
        ),
        check_vma=False,
    )
```

profile of v0, /device:TPU:0, one launch (start us, length us, event | category | flops | bytes accessed | tf_op | source)
XLA Modules:
  0.0 747.0 jit_solution(13027547879351057881)
XLA Ops:
  7.9 23.4 %all_gather.30 = f32[7,4096]{1,0:T(8,128)S(1)} all-gather(f32[7,256]{1,0:T(8,128)S(1)} %pad_maximum_fusion.9), channel_id=1, replica_groups=mesh['ia'=16,'ja'=2] {'ia'}, dimensions={1}, use_global_device_ids=true | all-gather | bytes 121856 | tf_op jit(solution)/shard_map/all_gather | solution.py:66
  31.3 4.4 all_gather.31
  35.7 54.4 %while.90 = (s32[]{:T(128)}, f32[6,512]{1,0:T(8,128)S(1)}, f32[6,4096]{1,0:T(8,128)S(1)}, s32[]{:T(128)}, s32[]{:T(128)}, /*index=5*/f32[7,4096]{1,0:T(8,128)S(1...) while((s32[]{:T(128)}, f32[6,512]{1,0:T(8,128)S(1)}, ...), condition=%wide.region_8.9_spmd, body=%wide.region_0.8_spmd.sunk | while | flops 9714969 | bytes 11740658 | solution.py:56
  91.6 6.4 reduce-scatter.11.cloned.1.call-done
  98.0 58.5 %reduce-scatter.13.cloned.1.call-done = f32[6,256]{1,0:T(8,128)} async-done(((f32[6,4096]{1,0:T(8,128)}), f32[6,256]{1,0:T(8,128)}) %reduce-scatter.13.cloned.1.call-update) | async-done | bytes 6160 | tf_op jit(solution)/shard_map/reduce_scatter | solution.py:78
  157.3 19.7 %all_gather.32 = f32[7,4096]{1,0:T(8,128)S(1)} all-gather(f32[7,256]{1,0:T(8,128)S(1)} %pad_maximum_fusion.8), channel_id=1, replica_groups=mesh['ia'=16,'ja'=2] {'ia'}, dimensions={1}, use_global_device_ids=true | all-gather | bytes 121856 | tf_op jit(solution)/shard_map/all_gather | solution.py:66
  177.1 4.4 all_gather.33
  181.4 54.4 %while.91 = (s32[]{:T(128)}, f32[6,512]{1,0:T(8,128)S(1)}, f32[6,4096]{1,0:T(8,128)S(1)}, s32[]{:T(128)}, s32[]{:T(128)}, /*index=5*/f32[7,4096]{1,0:T(8,128)S(1...) while((s32[]{:T(128)}, f32[6,512]{1,0:T(8,128)S(1)}, ...), condition=%wide.region_19.20_spmd, body=%wide.region_11.19_spmd.sunk | while | flops 9714969 | bytes 11740658 | solution.py:56
  237.1 6.6 reduce-scatter.15.cloned.1.call-done
  243.6 58.4 %reduce-scatter.17.cloned.1.call-done = f32[6,256]{1,0:T(8,128)} async-done(((f32[6,4096]{1,0:T(8,128)}), f32[6,256]{1,0:T(8,128)}) %reduce-scatter.17.cloned.1.call-update) | async-done | bytes 6160 | tf_op jit(solution)/shard_map/reduce_scatter | solution.py:78
  302.8 19.8 %all_gather.34 = f32[7,4096]{1,0:T(8,128)S(1)} all-gather(f32[7,256]{1,0:T(8,128)S(1)} %pad_maximum_fusion.7), channel_id=1, replica_groups=mesh['ia'=16,'ja'=2] {'ia'}, dimensions={1}, use_global_device_ids=true | all-gather | bytes 121856 | tf_op jit(solution)/shard_map/all_gather | solution.py:66
  322.6 4.4 all_gather.35
  327.0 54.0 %while.92 = (s32[]{:T(128)}, f32[6,512]{1,0:T(8,128)S(1)}, f32[6,4096]{1,0:T(8,128)S(1)}, s32[]{:T(128)}, s32[]{:T(128)}, /*index=5*/f32[7,4096]{1,0:T(8,128)S(1...) while((s32[]{:T(128)}, f32[6,512]{1,0:T(8,128)S(1)}, ...), condition=%wide.region_30.31_spmd, body=%wide.region_22.30_spmd.sunk | while | flops 9714969 | bytes 11740658 | solution.py:56
  382.2 6.5 reduce-scatter.19.cloned.1.call-done
  388.7 58.5 %reduce-scatter.21.cloned.1.call-done = f32[6,256]{1,0:T(8,128)} async-done(((f32[6,4096]{1,0:T(8,128)}), f32[6,256]{1,0:T(8,128)}) %reduce-scatter.21.cloned.1.call-update) | async-done | bytes 6160 | tf_op jit(solution)/shard_map/reduce_scatter | solution.py:78
  447.9 19.7 %all_gather.36 = f32[7,4096]{1,0:T(8,128)S(1)} all-gather(f32[7,256]{1,0:T(8,128)S(1)} %pad_maximum_fusion.6), channel_id=1, replica_groups=mesh['ia'=16,'ja'=2] {'ia'}, dimensions={1}, use_global_device_ids=true | all-gather | bytes 121856 | tf_op jit(solution)/shard_map/all_gather | solution.py:66
  467.7 4.4 all_gather.37
  472.1 54.6 %while.93 = (s32[]{:T(128)}, f32[6,512]{1,0:T(8,128)S(1)}, f32[6,4096]{1,0:T(8,128)S(1)}, s32[]{:T(128)}, s32[]{:T(128)}, /*index=5*/f32[7,4096]{1,0:T(8,128)S(1...) while((s32[]{:T(128)}, f32[6,512]{1,0:T(8,128)S(1)}, ...), condition=%wide.region_41.42_spmd, body=%wide.region_33.41_spmd.sunk | while | flops 9714969 | bytes 11740658 | solution.py:56
  473.5 1.9 conditional.13
  483.7 1.9 conditional.13
  487.2 1.9 conditional.13
  490.6 1.9 conditional.13
  494.0 1.9 conditional.13
  497.4 1.9 conditional.13
  507.6 1.9 conditional.13
  528.1 6.4 reduce-scatter.23.cloned.1.call-done
  534.5 58.6 %reduce-scatter.25.cloned.1.call-done = f32[6,256]{1,0:T(8,128)} async-done(((f32[6,4096]{1,0:T(8,128)}), f32[6,256]{1,0:T(8,128)}) %reduce-scatter.25.cloned.1.call-update) | async-done | bytes 6160 | tf_op jit(solution)/shard_map/reduce_scatter | solution.py:78
  593.8 19.8 %all_gather.38 = f32[7,4096]{1,0:T(8,128)S(1)} all-gather(f32[7,256]{1,0:T(8,128)S(1)} %pad_maximum_fusion.5), channel_id=1, replica_groups=mesh['ia'=16,'ja'=2] {'ia'}, dimensions={1}, use_global_device_ids=true | all-gather | bytes 121856 | tf_op jit(solution)/shard_map/all_gather | solution.py:66
  613.6 4.4 all_gather.39
  618.0 54.6 %while.94 = (s32[]{:T(128)}, f32[6,512]{1,0:T(8,128)S(1)}, f32[6,4096]{1,0:T(8,128)S(1)}, s32[]{:T(128)}, s32[]{:T(128)}, /*index=5*/f32[7,4096]{1,0:T(8,128)S(1...) while((s32[]{:T(128)}, f32[6,512]{1,0:T(8,128)S(1)}, ...), condition=%wide.region_52.53_spmd, body=%wide.region_44.52_spmd.sunk | while | flops 9714969 | bytes 11740658 | solution.py:56
  673.8 6.6 reduce-scatter.27.cloned.1.call-done
  680.4 58.4 %reduce-scatter.29.cloned.1.call-done = f32[6,256]{1,0:T(8,128)} async-done(((f32[6,4096]{1,0:T(8,128)}), f32[6,256]{1,0:T(8,128)}) %reduce-scatter.29.cloned.1.call-update) | async-done | bytes 6160 | tf_op jit(solution)/shard_map/reduce_scatter | solution.py:78
  (1267 shorter events, 369.1 us)
Async XLA Ops:
  7.2 90.8 %reduce-scatter.11.cloned.1.call-start = ((), (), s32[]{:S(2)}) async-start(), calls=%async_computation.10 | async-start | bytes 24576 | tf_op jit(solution)/shard_map/reduce_scatter | solution.py:79
  35.7 121.6 %copy-start.10 = (f32[3,256]{1,0:T(4,128)S(1)}, f32[3,256]{1,0:T(4,128)}, u32[]{:S(2)}) copy-start(f32[3,256]{1,0:T(4,128)} %param.24) | copy-start | bytes 9220
  35.7 121.6 %copy-start.11 = (f32[3,256]{1,0:T(4,128)S(1)}, f32[3,256]{1,0:T(4,128)}, u32[]{:S(2)}) copy-start(f32[3,256]{1,0:T(4,128)} %param.23) | copy-start | bytes 9220
  35.7 121.6 %copy-start.12 = (f32[256]{0:T(256)S(1)}, f32[256]{0:T(256)}, u32[]{:S(2)}) copy-start(f32[256]{0:T(256)} %param.25) | copy-start | bytes 3076
  90.2 0.6 copy-start.6
  90.2 0.7 copy-start.1
  90.8 65.8 %reduce-scatter.13.cloned.1.call-start = ((), (), s32[]{:S(2)}) async-start(), calls=%async_computation.11 | async-start | bytes 139264 | tf_op jit(solution)/shard_map/reduce_scatter | solution.py:78
  91.6 152.1 %reduce-scatter.15.cloned.1.call-start = ((), (), s32[]{:S(2)}) async-start(), calls=%async_computation.12 | async-start | bytes 24576 | tf_op jit(solution)/shard_map/reduce_scatter | solution.py:79
  235.8 0.6 copy-start.7
  235.8 0.7 copy-start.2
  236.5 65.6 %reduce-scatter.17.cloned.1.call-start = ((), (), s32[]{:S(2)}) async-start(), calls=%async_computation.13 | async-start | bytes 139264 | tf_op jit(solution)/shard_map/reduce_scatter | solution.py:78
  237.0 151.7 %reduce-scatter.19.cloned.1.call-start = ((), (), s32[]{:S(2)}) async-start(), calls=%async_computation.14 | async-start | bytes 24576 | tf_op jit(solution)/shard_map/reduce_scatter | solution.py:79
  381.0 0.6 copy-start.8
  381.0 0.7 copy-start.3
  381.6 65.6 %reduce-scatter.21.cloned.1.call-start = ((), (), s32[]{:S(2)}) async-start(), calls=%async_computation.15 | async-start | bytes 139264 | tf_op jit(solution)/shard_map/reduce_scatter | solution.py:78
  382.2 152.3 %reduce-scatter.23.cloned.1.call-start = ((), (), s32[]{:S(2)}) async-start(), calls=%async_computation.16 | async-start | bytes 24576 | tf_op jit(solution)/shard_map/reduce_scatter | solution.py:79
  526.7 0.6 copy-start.9
  526.7 0.7 copy-start.4
  527.3 65.7 %reduce-scatter.25.cloned.1.call-start = ((), (), s32[]{:S(2)}) async-start(), calls=%async_computation.17 | async-start | bytes 139264 | tf_op jit(solution)/shard_map/reduce_scatter | solution.py:78
  528.1 152.3 %reduce-scatter.27.cloned.1.call-start = ((), (), s32[]{:S(2)}) async-start(), calls=%async_computation.18 | async-start | bytes 24576 | tf_op jit(solution)/shard_map/reduce_scatter | solution.py:79
  672.5 0.6 copy-start.5
  672.6 0.7 copy-start
  673.2 65.6 %reduce-scatter.29.cloned.1.call-start = ((), (), s32[]{:S(2)}) async-start(), calls=%async_computation.19 | async-start | bytes 139264 | tf_op jit(solution)/shard_map/reduce_scatter | solution.py:78
Sparse Core Ops, SparseCore 0:
  90.9 7.0 reduce-scatter.10
  101.5 55.0 reduce-scatter.12
  236.6 7.0 reduce-scatter.14
  247.0 55.0 reduce-scatter.16
  381.7 6.9 reduce-scatter.18
  392.0 55.0 reduce-scatter.20
  527.5 6.9 reduce-scatter.22
  538.0 55.0 reduce-scatter.24
  673.3 7.0 reduce-scatter.26
  683.7 55.0 reduce-scatter.28
where the time goes:
time: 749 us; the launch traced here: 747 us
  waiting for transfers between devices  328 us (44%)
  other arithmetic  197 us (26%)
  blocking collectives  124 us (17%)
  loops' own time  54.6 us (7%)
  local copies, waits for them, and re-layouts  28.6 us (4%)
  between operations  14.5 us (2%)
    reduce_scatter x5, waiting for transfers between devices, evaluate(): col_total = lax.psum_scatter(col_acc, 'ia', scatter_dimension=1, tiled=True)  292 us
    all_gather x5, blocking collectives, evaluate(): col_set = lax.all_gather(packed, 'ia', axis=1, tiled=True)  102 us
    convert_element_type x80, other arithmetic, weigher(): return (row_index[:, None] < col_index[None, :]).astype(jnp.float32)  63.7 us
    another operation x5, loops' own time, tile_forces(): return lax.fori_loop(0, row_splits * col_splits, visit, start_acc)  50.9 us
    reduce_sum x80, other arithmetic, pair_block(): return (row_part, -jnp.sum(terms * row_set[6][None, :, None], 1))  45.1 us
    mul x80, other arithmetic, pair_block(): offset * cube  35.2 us
    reduce_scatter x5, waiting for transfers between devices, evaluate(): lax.psum_scatter(row_acc, 'ja', scatter_dimension=1, tiled=True) + col_total  32.4 us
    reduce_sum x80, other arithmetic, pair_block(): square = jnp.sum(offset * offset, 0) + soft_square  29.4 us
  transfers between devices with their start and end apart: 10, of which 10 were waited for; matrix products, arithmetic and copies ran while one was open for 0% of the time, Pallas kernels for 0%

commit v1 on v0

v1 whole, which is shorter than its diff:
```python
import functools

import jax
import jax.numpy as jnp
from jax import lax
from jax.experimental import pallas as pl
from jax.experimental.pallas import tpu as pltpu
from jax.sharding import PartitionSpec as P

STEPS = 4
GROUP = 4
ROWS = 32
LANES = 128

soft_square = 0.0025
time_step = 0.03125

MESH = pl.DeviceIdType.MESH


def round_bf16(x):
    return x.astype(jnp.bfloat16).astype(jnp.float32)


def spread_rows(state, rows_ref):
    n = state.shape[1]
    turned = state.T
    for q in range(6):
        rows_ref[q] = jnp.broadcast_to(turned[:, q : q + 1], (n, LANES))


def source_sides(block):
    mass = block[6:7]
    n = block.shape[1]
    part = lax.broadcasted_iota(jnp.int32, (8, n), 0)
    full = jnp.where(part == 6, mass, block * mass)
    full = jnp.where(part == 7, 0.0, full)
    first = round_bf16(full)
    rest = full - first
    second = round_bf16(rest)
    third = rest - second
    stacked = jnp.concatenate([first, second, third, jnp.zeros_like(full)], 0)
    return stacked.astype(jnp.bfloat16)


def pair_tiles(block_ref, rows_ref, w_ref, v_ref, side_ref, slots, own):
    n = rows_ref.shape[1]
    depth = slots * n
    for k in range(slots):
        side = source_sides(block_ref[k])
        side_ref[:, k * n : (k + 1) * n] = side
        side_ref[:, depth + k * n : depth + (k + 1) * n] = side

    def row_tile(r, carry):
        start = pl.multiple_of(r * ROWS, ROWS)
        here = [rows_ref[q, pl.ds(start, ROWS), :] for q in range(6)]
        for k in range(slots):
            for c in range(n // LANES):
                lanes = slice(c * LANES, (c + 1) * LANES)
                there = [block_ref[k, q : q + 1, lanes] for q in range(6)]
                off = [there[q] - here[q] for q in range(3)]
                clo = [there[q + 3] - here[q + 3] for q in range(3)]
                square = off[0] * off[0] + off[1] * off[1] + (off[2] * off[2] + soft_square)
                dot = off[0] * clo[0] + off[1] * clo[1] + off[2] * clo[2]
                inverse = lax.rsqrt(square)
                inv2 = inverse * inverse
                w = inv2 * inverse
                if own and k == 0:
                    row_at = lax.broadcasted_iota(jnp.int32, (ROWS, LANES), 0) + start
                    col_at = lax.broadcasted_iota(jnp.int32, (ROWS, LANES), 1) + c * LANES
                    w = jnp.where(row_at == col_at, 0.0, w)
                v = w * (inv2 * dot)
                at = k * n + c * LANES
                for ref, val in ((w_ref, w), (v_ref, v)):
                    high = val.astype(jnp.bfloat16)
                    low = (val - high.astype(jnp.float32)).astype(jnp.bfloat16)
                    ref[pl.ds(start, ROWS), at : at + LANES] = high
                    ref[pl.ds(start, ROWS), depth + at : depth + at + LANES] = low
        return carry

    lax.fori_loop(0, n // ROWS, row_tile, 0)


def contract(side_ref, pair_ref):
    return lax.dot_general(
        side_ref[...], pair_ref[...], (((1,), (1,)), ((), ())), preferred_element_type=jnp.float32
    )


def fold(total):
    return total[0:8] + total[8:16] + total[16:24]


def finish(state, w_sum, v_sum):
    pos, vel = state[0:3], state[3:6]
    ws, vs = fold(w_sum), fold(v_sum)
    accel = ws[0:3] - pos * ws[6:7]
    jerk = (ws[3:6] - vel * ws[6:7]) - 3.0 * (vs[0:3] - pos * vs[6:7])
    return accel, jerk


def kernel(
    axes, sizes, pos_ref, vel_ref, mass_ref, opos_ref, ovel_ref, oacc_ref, ojerk_ref,
    gath, rows, w_buf, v_buf, side, w_sum, v_sum, send_sem, recv_sem,
):
    nia, nja = sizes
    devices = nia * nja
    slots = min(GROUP, devices)
    groups = devices // slots
    ia, ja = lax.axis_index(axes[0]), lax.axis_index(axes[1])

    def partner(t):
        return ((ia + t // nja) % nia, (ja + t % nja) % nja)

    barrier = pltpu.get_barrier_semaphore()

    def greet(t, carry):
        pl.semaphore_signal(barrier, inc=1, device_id=partner(t), device_id_type=MESH)
        return carry

    lax.fori_loop(1, devices, greet, 0)
    pl.semaphore_wait(barrier, devices - 1)

    def copy(par, t):
        return pltpu.make_async_remote_copy(
            src_ref=gath.at[par, 0],
            dst_ref=gath.at[par, t],
            send_sem=send_sem.at[par, t],
            recv_sem=recv_sem.at[par, t],
            device_id=partner(t),
            device_id_type=MESH,
        )

    def forces(par, pos, vel):
        state = jnp.concatenate([pos, vel, mass_ref[...], jnp.zeros_like(mass_ref)], 0)
        gath[par, 0] = state

        def begin(t, carry):
            copy(par, t).start()
            return carry

        lax.fori_loop(1, devices, begin, 0)
        spread_rows(state, rows)
        w_sum[...] = jnp.zeros_like(w_sum)
        v_sum[...] = jnp.zeros_like(v_sum)

        def group(g, own):
            start = g * slots
            for k in range(slots):
                if not (own and k == 0):
                    copy(par, start + k).wait_recv()
            pair_tiles(gath.at[par, pl.ds(start, slots)], rows, w_buf, v_buf, side, slots, own)
            w_sum[...] += contract(side, w_buf)
            v_sum[...] += contract(side, v_buf)

        group(0, True)

        def later(g, carry):
            group(g, False)
            return carry

        lax.fori_loop(1, groups, later, 0)

        def finish_send(t, carry):
            copy(par, t).wait_send()
            return carry

        lax.fori_loop(1, devices, finish_send, 0)
        return finish(state, w_sum[...], v_sum[...])

    pos, vel = pos_ref[...], vel_ref[...]
    step_sq = time_step * time_step
    accel, jerk = forces(0, pos, vel)
    opos_ref[...] = pos
    ovel_ref[...] = vel
    oacc_ref[...] = accel
    ojerk_ref[...] = jerk

    def step(index, carry):
        position, velocity = opos_ref[...], ovel_ref[...]
        accel, jerk = oacc_ref[...], ojerk_ref[...]
        predicted_pos = (
            position
            + time_step * velocity
            + step_sq / 2.0 * accel
            + step_sq * time_step / 6.0 * jerk
        )
        predicted_vel = velocity + time_step * accel + step_sq / 2.0 * jerk
        new_accel, new_jerk = forces((index + 1) % 2, predicted_pos, predicted_vel)
        new_velocity = (
            velocity + time_step / 2.0 * (accel + new_accel) + step_sq / 12.0 * (jerk - new_jerk)
        )
        opos_ref[...] = (
            position
            + time_step / 2.0 * (velocity + new_velocity)
            + step_sq / 12.0 * (accel - new_accel)
        )
        ovel_ref[...] = new_velocity
        oacc_ref[...] = new_accel
        ojerk_ref[...] = new_jerk
        return carry

    lax.fori_loop(0, STEPS, step, 0)


def per_device(axes, sizes, position, velocity, mass):
    n = position.shape[1]
    devices = sizes[0] * sizes[1]
    depth = 2 * min(GROUP, devices) * n
    vmem = pl.BlockSpec(memory_space=pltpu.VMEM)
    shape = jax.ShapeDtypeStruct(position.shape, jnp.float32)
    return tuple(
        pl.pallas_call(
            functools.partial(kernel, axes, sizes),
            out_shape=(shape,) * 4,
            in_specs=[vmem] * 3,
            out_specs=(vmem,) * 4,
            scratch_shapes=[
                pltpu.VMEM((2, devices, 8, n), jnp.float32),
                pltpu.VMEM((6, n, LANES), jnp.float32),
                pltpu.VMEM((n, depth), jnp.bfloat16),
                pltpu.VMEM((n, depth), jnp.bfloat16),
                pltpu.VMEM((32, depth), jnp.bfloat16),
                pltpu.VMEM((32, n), jnp.float32),
                pltpu.VMEM((32, n), jnp.float32),
                pltpu.SemaphoreType.DMA((2, devices)),
                pltpu.SemaphoreType.DMA((2, devices)),
            ],
            compiler_params=pltpu.CompilerParams(
                collective_id=0, has_side_effects=True, vmem_limit_bytes=40 * 1024 * 1024
            ),
        )(position, velocity, mass[None, :])
    )


def solution(mesh):
    axes = ("ia", "ja")
    sizes = (mesh.shape["ia"], mesh.shape["ja"])
    split = P(None, axes)
    return jax.shard_map(
        functools.partial(per_device, axes, sizes),
        mesh=mesh,
        in_specs=(split, split, P(axes)),
        out_specs=(split,) * 4,
        check_vma=False,
    )
```

time: 749 us -> 106 us (0.14)
  waiting for transfers between devices: 328 us -> 0 us
  other arithmetic: 197 us -> 0 us
  blocking collectives: 124 us -> 0 us
  Pallas kernels: 0 us -> 101 us
  loops' own time: 54.6 us -> 0 us
  local copies, waits for them, and re-layouts: 28.6 us -> 4.42 us
  between operations: 14.5 us -> 0.65 us
    reduce_scatter x10 -> x0, waiting for transfers between devices: 325 us -> none  [the longest x5 292 us: evaluate(): col_total = lax.psum_scatter(col_acc, 'ia', scatter_dimension=1, tiled=True)]
    all_gather x10 -> x0, blocking collectives: 124 us -> none  [the longest x5 102 us: evaluate(): col_set = lax.all_gather(packed, 'ia', axis=1, tiled=True)]
    pallas_call x0 -> x1, Pallas kernels: none -> 101 us  [per_device(): pl.pallas_call(functools.partial(kernel, axes, sizes), out_shape=(shape,)...]
    reduce_sum x160 -> x0, other arithmetic: 74.5 us -> none  [the longest x80 45.1 us: pair_block(): return (row_part, -jnp.sum(terms * row_set[6][None, :, None], 1))]
    convert_element_type x80 -> x0, other arithmetic: 63.7 us -> none  [weigher(): return (row_index[:, None] < col_index[None, :]).astype(jnp.float32)]
    another operation x85 -> x0, loops' own time: 54.6 us -> none  [the longest x5 50.9 us: tile_forces(): return lax.fori_loop(0, row_splits * col_splits, visit, start_acc)]
    mul x160 -> x0, other arithmetic: 49.7 us -> none  [the longest x80 35.2 us: pair_block(): offset * cube]
    slice x320 -> x0, local copies, waits for them, and re-layouts: 25.6 us -> none  [the longest x160 12.9 us: pair_block(): closing = col_set[3:6, None, :] - row_set[3:6, :, None]]
  transfers between devices with their start and end apart: 10 -> 0, of which waited for: 10 -> 0; matrix products, arithmetic and copies ran while one was open for 0% -> 0% of each run, Pallas kernels for 0% -> 0%
where the time goes in v1:
time: 106 us
  Pallas kernels  101 us (95%)
  local copies, waits for them, and re-layouts  4.42 us (4%)
    pallas_call x1, Pallas kernels, per_device(): pl.pallas_call(functools.partial(kernel, axes, sizes), out_shape=(shape,)...  101 us
    unnamed x10, local copies, waits for them, and re-layouts  4.42 us

profile of v1, /device:TPU:0, one launch (start us, length us, event | category | flops | bytes accessed | tf_op | source)
XLA Modules:
  0.0 106.1 jit_solution(2234841678003522362)
XLA Ops:
  0.6 0.0 copy-start.2
  0.6 0.7 copy-done.2
  1.3 0.0 copy-start
  1.3 0.7 copy-done
  2.0 0.0 copy-start.1
  2.0 0.7 copy-done.1
  2.7 101.0 %shard_map.66 = (f32[3,256]{1,0:T(4,128)S(1)}, f32[3,256]{1,0:T(4,128)S(1)}, f32[3,256]{1,0:T(4,128)S(1)}, f32[3,256]{1,0:T(4,128)S(1)}) custom-call(f32[3,256]{1,0:T(4,128)S(1)} %copy-done, f32[3,256]{1,0:T(4,128)S(1)} %copy-done.1, f32[1,256]{1,0:T(1,128)S(1)} %bitcast.1), custom_call_target="tpu_custom_call" | custom-call | tf_op jit(solution)/shard_map/pallas_call | solution.py:213
  103.7 0.6 copy.11
  104.3 0.6 copy.12
  104.9 0.6 copy.13
  105.5 0.6 copy.14
Async XLA Ops:
  0.6 0.7 copy-start.2
  1.3 0.7 copy-start
  2.0 0.7 copy-start.1

commit v2 on v1

--- a/solution.py
+++ b/solution.py
@@ -9,7 +9,7 @@
 
 STEPS = 4
 GROUP = 4
-ROWS = 32
+ROWS = 256
 LANES = 128
 
 soft_square = 0.0025
@@ -43,7 +43,7 @@
     return stacked.astype(jnp.bfloat16)
 
 
-def pair_tiles(block_ref, rows_ref, w_ref, v_ref, side_ref, slots, own):
+def pair_tiles(block_ref, rows_ref, pair_ref, side_ref, slots, own):
     n = rows_ref.shape[1]
     depth = slots * n
     for k in range(slots):
@@ -54,6 +54,7 @@
     def row_tile(r, carry):
         start = pl.multiple_of(r * ROWS, ROWS)
         here = [rows_ref[q, pl.ds(start, ROWS), :] for q in range(6)]
+        tiles = [[], [], [], []]
         for k in range(slots):
             for c in range(n // LANES):
                 lanes = slice(c * LANES, (c + 1) * LANES)
@@ -70,21 +71,19 @@
                     col_at = lax.broadcasted_iota(jnp.int32, (ROWS, LANES), 1) + c * LANES
                     w = jnp.where(row_at == col_at, 0.0, w)
                 v = w * (inv2 * dot)
-                at = k * n + c * LANES
-                for ref, val in ((w_ref, w), (v_ref, v)):
+                for at, val in ((0, w), (2, v)):
                     high = val.astype(jnp.bfloat16)
-                    low = (val - high.astype(jnp.float32)).astype(jnp.bfloat16)
-                    ref[pl.ds(start, ROWS), at : at + LANES] = high
-                    ref[pl.ds(start, ROWS), depth + at : depth + at + LANES] = low
+                    tiles[at].append(high)
+                    tiles[at + 1].append((val - high.astype(jnp.float32)).astype(jnp.bfloat16))
+        for at in range(2):
+            high = jnp.concatenate(tiles[2 * at], 1)
+            low = jnp.concatenate(tiles[2 * at + 1], 1)
+            both = jnp.concatenate([high, low], 1)
+            got = lax.dot_general(both, side_ref[...], (((1,), (1,)), ((), ())), preferred_element_type=jnp.float32)
+            pair_ref[pl.ds(start + at * n, ROWS), :] += got
         return carry
 
     lax.fori_loop(0, n // ROWS, row_tile, 0)
-
-
-def contract(side_ref, pair_ref):
-    return lax.dot_general(
-        side_ref[...], pair_ref[...], (((1,), (1,)), ((), ())), preferred_element_type=jnp.float32
-    )
 
 
 def fold(total):
@@ -101,7 +100,7 @@
 
 def kernel(
     axes, sizes, pos_ref, vel_ref, mass_ref, opos_ref, ovel_ref, oacc_ref, ojerk_ref,
-    gath, rows, w_buf, v_buf, side, w_sum, v_sum, send_sem, recv_sem,
+    gath, rows, side, sums, send_sem, recv_sem,
 ):
     nia, nja = sizes
     devices = nia * nja
@@ -141,17 +140,14 @@
 
         lax.fori_loop(1, devices, begin, 0)
         spread_rows(state, rows)
-        w_sum[...] = jnp.zeros_like(w_sum)
-        v_sum[...] = jnp.zeros_like(v_sum)
+        sums[...] = jnp.zeros_like(sums)
 
         def group(g, own):
             start = g * slots
             for k in range(slots):
                 if not (own and k == 0):
                     copy(par, start + k).wait_recv()
-            pair_tiles(gath.at[par, pl.ds(start, slots)], rows, w_buf, v_buf, side, slots, own)
-            w_sum[...] += contract(side, w_buf)
-            v_sum[...] += contract(side, v_buf)
+            pair_tiles(gath.at[par, pl.ds(start, slots)], rows, sums, side, slots, own)
 
         group(0, True)
 
@@ -166,7 +162,7 @@
             return carry
 
         lax.fori_loop(1, devices, finish_send, 0)
-        return finish(state, w_sum[...], v_sum[...])
+        return finish(state, sums[: pos.shape[1], :].T, sums[pos.shape[1] :, :].T)
 
     pos, vel = pos_ref[...], vel_ref[...]
     step_sq = time_step * time_step
@@ -218,11 +214,8 @@
             scratch_shapes=[
                 pltpu.VMEM((2, devices, 8, n), jnp.float32),
                 pltpu.VMEM((6, n, LANES), jnp.float32),
-                pltpu.VMEM((n, depth), jnp.bfloat16),
-                pltpu.VMEM((n, depth), jnp.bfloat16),
                 pltpu.VMEM((32, depth), jnp.bfloat16),
-                pltpu.VMEM((32, n), jnp.float32),
-                pltpu.VMEM((32, n), jnp.float32),
+                pltpu.VMEM((2 * n, 32), jnp.float32),
                 pltpu.SemaphoreType.DMA((2, devices)),
                 pltpu.SemaphoreType.DMA((2, devices)),
             ],

time: 106 us -> 82.8 us (0.78)
  Pallas kernels: 101 us -> 77.5 us
    pallas_call x1, Pallas kernels: 101 us -> 77.5 us  [per_device(): pl.pallas_call(functools.partial(kernel, axes, sizes), out_shape=(shape,)...]
where the time goes in v2:
time: 82.8 us; the launch traced here: 82.6 us
  Pallas kernels  77.5 us (94%)
  local copies, waits for them, and re-layouts  4.42 us (5%)
    pallas_call x1, Pallas kernels, per_device(): pl.pallas_call(functools.partial(kernel, axes, sizes), out_shape=(shape,)...  77.5 us
    unnamed x10, local copies, waits for them, and re-layouts  4.42 us

profile of v2, /device:TPU:0, one launch (start us, length us, event | category | flops | bytes accessed | tf_op | source)
XLA Modules:
  0.0 82.6 jit_solution(1315604570111838297)
XLA Ops:
  0.6 0.0 copy-start.2
  0.6 0.7 copy-done.2
  1.3 0.0 copy-start
  1.3 0.7 copy-done
  2.0 0.0 copy-start.1
  2.0 0.7 copy-done.1
  2.7 77.5 %shard_map.66 = (f32[3,256]{1,0:T(4,128)S(1)}, f32[3,256]{1,0:T(4,128)S(1)}, f32[3,256]{1,0:T(4,128)S(1)}, f32[3,256]{1,0:T(4,128)S(1)}) custom-call(f32[3,256]{1,0:T(4,128)S(1)} %copy-done, f32[3,256]{1,0:T(4,128)S(1)} %copy-done.1, f32[1,256]{1,0:T(1,128)S(1)} %bitcast.1), custom_call_target="tpu_custom_call" | custom-call | tf_op jit(solution)/shard_map/pallas_call | solution.py:209
  80.2 0.6 copy.11
  80.8 0.6 copy.12
  81.4 0.6 copy.13
  82.0 0.6 copy.14
Async XLA Ops:
  0.6 0.7 copy-start.2
  1.3 0.7 copy-start
  2.0 0.7 copy-start.1

commit v3 on v2

--- a/solution.py
+++ b/solution.py
@@ -9,7 +9,6 @@
 
 STEPS = 4
 GROUP = 4
-ROWS = 256
 LANES = 128
 
 soft_square = 0.0025
@@ -43,19 +42,28 @@
     return stacked.astype(jnp.bfloat16)
 
 
-def pair_tiles(block_ref, rows_ref, pair_ref, side_ref, slots, own):
+def pair_tiles(block_ref, rows_ref, pair_ref, side_ref, slots, own, arrive):
     n = rows_ref.shape[1]
     depth = slots * n
-    for k in range(slots):
+    ROWS = n
+
+    def prepare(k):
         side = source_sides(block_ref[k])
         side_ref[:, k * n : (k + 1) * n] = side
         side_ref[:, depth + k * n : depth + (k + 1) * n] = side
 
+    if not own:
+        for k in range(slots):
+            prepare(k)
+
     def row_tile(r, carry):
-        start = pl.multiple_of(r * ROWS, ROWS)
+        start = r * ROWS
         here = [rows_ref[q, pl.ds(start, ROWS), :] for q in range(6)]
         tiles = [[], [], [], []]
         for k in range(slots):
+            if own:
+                arrive(k)
+                prepare(k)
             for c in range(n // LANES):
                 lanes = slice(c * LANES, (c + 1) * LANES)
                 there = [block_ref[k, q : q + 1, lanes] for q in range(6)]
@@ -83,7 +91,7 @@
             pair_ref[pl.ds(start + at * n, ROWS), :] += got
         return carry
 
-    lax.fori_loop(0, n // ROWS, row_tile, 0)
+    row_tile(0, 0)
 
 
 def fold(total):
@@ -144,10 +152,15 @@
 
         def group(g, own):
             start = g * slots
-            for k in range(slots):
+
+            def arrive(k):
                 if not (own and k == 0):
                     copy(par, start + k).wait_recv()
-            pair_tiles(gath.at[par, pl.ds(start, slots)], rows, sums, side, slots, own)
+
+            if not own:
+                for k in range(slots):
+                    arrive(k)
+            pair_tiles(gath.at[par, pl.ds(start, slots)], rows, sums, side, slots, own, arrive)
 
         group(0, True)
 

time: 82.8 us -> 82.6 us (level)
  no operation moved by 1% of the time
where the time goes in v3:
time: 82.6 us; the launch traced here: 82.4 us
  Pallas kernels  77.3 us (94%)
  local copies, waits for them, and re-layouts  4.42 us (5%)
    pallas_call x1, Pallas kernels, per_device(): pl.pallas_call(functools.partial(kernel, axes, sizes), out_shape=(shape,)...  77.3 us
    unnamed x10, local copies, waits for them, and re-layouts  4.42 us

profile of v3, /device:TPU:0, one launch (start us, length us, event | category | flops | bytes accessed | tf_op | source)
XLA Modules:
  0.0 82.4 jit_solution(13928720673977044004)
XLA Ops:
  0.6 0.0 copy-start.2
  0.6 0.7 copy-done.2
  1.3 0.0 copy-start
  1.3 0.7 copy-done
  2.0 0.0 copy-start.1
  2.0 0.7 copy-done.1
  2.7 77.3 %shard_map.66 = (f32[3,256]{1,0:T(4,128)S(1)}, f32[3,256]{1,0:T(4,128)S(1)}, f32[3,256]{1,0:T(4,128)S(1)}, f32[3,256]{1,0:T(4,128)S(1)}) custom-call(f32[3,256]{1,0:T(4,128)S(1)} %copy-done, f32[3,256]{1,0:T(4,128)S(1)} %copy-done.1, f32[1,256]{1,0:T(1,128)S(1)} %bitcast.1), custom_call_target="tpu_custom_call" | custom-call | tf_op jit(solution)/shard_map/pallas_call | solution.py:222
  80.0 0.6 copy.11
  80.6 0.6 copy.12
  81.2 0.6 copy.13
  81.8 0.6 copy.14
Async XLA Ops:
  0.6 0.7 copy-start.2
  1.3 0.7 copy-start
  2.0 0.7 copy-start.1
